TPU v7x, 512 devices: a whole 4x4x16 slice. The times are simulated.
512 devices in a mesh: seq: 8 (over y, core), head: 64 (over z, x).
Axes of the slice: x: 4, y: 4, z: 16, core: 2. Of those that a mesh axis runs over, the one named last changes fastest.
Arguments:
- tokens: bfloat16 [8192, 2048], P('seq', 'head'), may hold values from -6 to 6
- z_weight: bfloat16 [2048, 4096], P(None, 'head'), may hold values from -0.125 to 0.125
- x_weight: bfloat16 [2048, 4096], P(None, 'head'), may hold values from -0.79549513 to 0.79549513
- bc_weight: bfloat16 [2048, 256], replicated, may hold values from -0.125 to 0.125
- step_weight: bfloat16 [2048, 64], P(None, 'head'), may hold values from -0.125 to 0.125
- x_kernel: float32 [4, 4096], P(None, 'head'), may hold values from -3 to 3
- bc_kernel: float32 [4, 256], replicated, may hold values from -3 to 3
- step_bias: float32 [64], P('head'), may hold values from -9 to -3
- log_decay: float32 [64], P('head'), may hold values from 0 to 1.5
- skip_gain: float32 [64], P('head'), may hold values from 0.2 to 0.8
- norm_gain: bfloat16 [4096], P('head'), may hold values from 0.099609375 to 1.8984375
- out_weight: bfloat16 [4096, 2048], P('head'), may hold values from -0.09375 to 0.09375
Outputs:
- mixed: bfloat16 [8192, 2048], P('seq', 'head')
All inputs are finite; a program needn't handle non-finite values.
Results may differ from a plain program's by a relative error of at most 0.017.
Values may be sent and summed in bfloat16 or wider, within the bound.
A program may use at most 64 MiB of HBM per device.

v0:
```python
import jax
import jax.numpy as jnp
from jax import lax
from jax.sharding import PartitionSpec as P

CH = 256


def from_behind(block, axis, distance):
    devices = range(lax.axis_size(axis))
    route = [(i - distance, i) for i in devices if i - distance in devices]
    return lax.ppermute(block, axis, route)


def causal(padded, kernel):
    length = padded.shape[0] - 3
    total = kernel[0] * padded[0:length].astype(jnp.float32)
    for offset in range(1, 4):
        total = total + kernel[offset] * padded[offset : offset + length].astype(jnp.float32)
    return jax.nn.silu(total).astype(jnp.bfloat16)


def body(
    tokens,
    z_weight,
    x_weight,
    bc_weight,
    step_weight,
    x_kernel,
    bc_kernel,
    step_bias,
    log_decay,
    skip_gain,
    norm_gain,
    out_weight,
):
    tok_rows = tokens.shape[0]
    heads_here = step_bias.shape[0]
    inner_width = x_weight.shape[1]
    head_size = inner_width // heads_here
    state_size = bc_weight.shape[1] // 2
    piece = lax.all_gather(tokens, "head", axis=1, tiled=True)

    def product(weight):
        return jnp.dot(piece, weight, preferred_element_type=jnp.float32)

    z_sum = product(z_weight)
    x_sum = product(x_weight)
    bc_sum = product(bc_weight)
    step_raw = product(step_weight)
    z_in = z_sum.astype(jnp.bfloat16)
    x_in = x_sum.astype(jnp.bfloat16)
    bc_in = bc_sum.astype(jnp.bfloat16)
    border = jnp.concatenate([x_in[-3:], bc_in[-3:]], axis=1)
    border = from_behind(border, "seq", 1)
    x_conv = causal(jnp.concatenate([border[:, :inner_width], x_in], axis=0), x_kernel)
    bc_conv = causal(jnp.concatenate([border[:, inner_width:], bc_in], axis=0), bc_kernel)
    blocks = tok_rows // CH
    b_map = bc_conv[:, :state_size].reshape(blocks, CH, state_size)
    c_map = bc_conv[:, state_size:].reshape(blocks, CH, state_size)
    step_size = jax.nn.softplus(step_raw + step_bias)
    rate = -jnp.exp(log_decay) * step_size
    values = x_conv.reshape(blocks, CH, heads_here, head_size)
    steps_b = step_size.reshape(blocks, CH, heads_here)
    cumulative = jnp.cumsum(rate.reshape(blocks, CH, heads_here), axis=1)
    lower = (jnp.arange(CH)[:, None] >= jnp.arange(CH)[None, :])[None, :, :, None]
    gram = jnp.einsum("ctn,csn->cts", c_map, b_map, preferred_element_type=jnp.float32)
    spread = cumulative[:, :, None, :] - cumulative[:, None, :, :]
    mixing = jnp.where(
        lower,
        gram[..., None] * jnp.exp(jnp.where(lower, spread, 0.0)) * steps_b[:, None, :, :],
        0.0,
    ).astype(jnp.bfloat16)
    intra = jnp.einsum("ctsh,cshp->cthp", mixing, values, preferred_element_type=jnp.float32)
    tails = jnp.exp(cumulative[:, -1:, :] - cumulative) * steps_b
    weighted = (values.astype(jnp.float32) * tails[..., None]).astype(jnp.bfloat16)
    local = jnp.einsum("cthp,ctn->chpn", weighted, b_map, preferred_element_type=jnp.float32)
    block_decay = jnp.exp(cumulative[:, -1, :])

    def advance(carry, item):
        state, decay = carry
        term, factor = item
        return ((factor[:, None, None] * state + term, decay * factor), (state, decay))

    zero_state = jnp.zeros((heads_here, head_size, state_size), jnp.float32)
    unit_decay = jnp.ones((heads_here,), jnp.float32)
    (shard_state, shard_decay), (local_in, decay_in) = lax.scan(
        advance, (zero_state, unit_decay), (local, block_decay)
    )

    def relay(index, carried):
        return from_behind(shard_decay[:, None, None] * carried + shard_state, "seq", 1)

    incoming = lax.fori_loop(0, lax.axis_size("seq") - 1, relay, zero_state)
    entering = local_in + decay_in[:, :, None, None] * incoming[None]
    held = entering.astype(jnp.bfloat16)
    from_state = (
        jnp.einsum("ctn,chpn->cthp", c_map, held, preferred_element_type=jnp.float32)
        * jnp.exp(cumulative)[..., None]
    )
    output_y = intra + from_state + skip_gain[None, None, :, None] * values.astype(jnp.float32)
    gated = (
        output_y.reshape(tok_rows, inner_width) * jax.nn.silu(z_in.astype(jnp.float32))
    ).astype(jnp.bfloat16)
    head_count = lax.axis_size("head")
    columns = lax.all_to_all(out_weight, "head", split_axis=1, concat_axis=0, tiled=True)
    gain_row = norm_gain.reshape(1, inner_width)
    section = lax.all_gather(gated, "head", axis=1, tiled=True)
    gain_part = lax.all_gather(gain_row, "head", axis=1, tiled=True)
    section_f = section.astype(jnp.float32)
    scaled = (section_f * gain_part.astype(jnp.float32)).astype(jnp.bfloat16)
    partial_out = jnp.dot(scaled, columns, preferred_element_type=jnp.float32)
    squares = jnp.sum(section_f * section_f, axis=1)
    meansq = squares / (inner_width * head_count)
    return (partial_out * lax.rsqrt(meansq + 1e-05)[:, None]).astype(jnp.bfloat16)


def solution(mesh):
    placed = (
        P("seq", "head"),
        P(None, "head"),
        P(None, "head"),
        P(),
        P(None, "head"),
        P(None, "head"),
        P(),
        P("head"),
        P("head"),
        P("head"),
        P("head"),
        P("head", None),
    )
    return jax.shard_map(
        body, mesh=mesh, in_specs=placed, out_specs=P("seq", "head"), check_vma=False
    )
```

profile of v0, /device:TPU:10, one launch (start us, length us, event | category | flops | bytes accessed | tf_op | source)
XLA Modules:
  0.0 403.9 jit_solution(2700277313001061849)
XLA Ops:
  6.5 0.7 all-gather.4.cloned.1.call-update
  9.4 0.8 slice_bitcast_fusion.4
  10.2 0.8 fusion.44
  11.0 148.9 %all-gather.4.cloned.1.call-done = bf16[1024,2048]{0,1:T(8,128)(2,1)} async-done(((bf16[1024,32]{0,1:T(8,128)(2,1)}), bf16[1024,2048]{0,1:T(8,128)(2,1)}) %all-gather.4.cloned.1.call-update) | async-done | bytes 4194320 | tf_op jit(solution)/shard_map/all_gather | solution.py:42
  160.0 2.8 fusion.45
  162.8 1.2 reduce-window.6
  164.3 3.6 convolution_convert_fusion
  168.0 0.9 convolution_convert_fusion.2
  169.0 1.9 collective-permute-start.1
  171.3 3.5 collective-permute-done.1
  174.8 1.0 multiply_convert_fusion
  176.2 0.3 convert_multiply_fusion.2
  176.8 8.1 %while.28 = (s32[]{:T(128)}, f32[1,64,128]{2,1,0:T(8,128)S(1)}, f32[1]{0:T(128)}, f32[4,1,64,128]{3,2,1,0:T(8,128)S(1)}, f32[4,1]{0,1:T(1,128)S(1)}, /*index=5*/...) while((s32[]{:T(128)}, f32[1,64,128]{2,1,0:T(8,128)S(1)}, f32[1]{0:T(128)}, ...), condition=%wide.region_3.4_spmd.clone, body=%wide.region_2.3_spmd.clone.sunk | while | flops 32772 | bytes 164008 | solution.py:87
  176.8 0.6 constant_dynamic-slice_fusion.2
  177.4 0.7 bitcast_add_fusion.4
  178.8 0.6 constant_dynamic-slice_fusion.2
  179.4 0.7 bitcast_add_fusion.4
  180.8 0.6 constant_dynamic-slice_fusion.2
  181.4 0.7 bitcast_add_fusion.4
  182.8 0.6 constant_dynamic-slice_fusion.2
  183.4 0.7 bitcast_add_fusion.4
  184.8 0.5 fusion.10
  185.4 36.8 %while.27 = (s32[]{:T(128)}, f32[1,64,128]{2,1,0:T(8,128)S(1)}, f32[1]{0:T(128)}, f32[1,64,128]{2,1,0:T(8,128)S(1)}, s32[]{:T(128)}) while((s32[]{:T(128)}, f32[1,64,128]{2,1,0:T(8,128)S(1)}, f32[1]{0:T(128)}, f32[1,64,128]{2,1,0:T(8,128)S(1)}, s32[]{:T(128)}) %tuple.53), condition=%wide.region_5.6_spmd, body=%wide.region_4.5_spmd.sunk | while | flops 16386 | bytes 229481 | solution.py:94
  185.4 2.1 collective-permute-start
  187.5 3.3 collective-permute-done
  190.8 1.9 collective-permute-start
  192.7 3.3 collective-permute-done
  196.0 1.9 collective-permute-start
  198.0 3.3 collective-permute-done
  201.3 1.9 collective-permute-start
  203.2 3.3 collective-permute-done
  206.5 1.9 collective-permute-start
  208.4 3.3 collective-permute-done
  211.7 1.9 collective-permute-start
  213.7 3.3 collective-permute-done
  217.0 1.9 collective-permute-start
  218.9 3.3 collective-permute-done
  222.7 3.7 multiply_convert_fusion.1
  226.5 0.3 copy.63
  226.8 1.0 reshape.305
  227.8 10.3 %all-to-all-start = ((bf16[64,2,1024]{2,1,0:T(2,128)(2,1)}), bf16[64,2,1024]{2,1,0:T(2,128)(2,1)S(1)}, u32[]{:S(2)}, u32[]{:S(2)}) async-start(bf16[64,2,1024]{2,1,0:T(2,128)(2,1)} %reshape.305), calls=%async_computation | async-start | bytes 524288 | tf_op jit(solution)/shard_map/all_to_all | solution.py:106
  238.1 1.3 dynamic-slice
  240.3 147.3 %all-reduce = bf16[4096]{0:T(1024)(128)(2,1)S(1)} all-reduce(bf16[4096]{0:T(1024)(128)(2,1)S(1)} %dynamic-update-slice), channel_id=2, replica_groups=mesh['seq'=8,'head'=64] {'head'}, use_global_device_ids=true, to_apply=%add | all-reduce | flops 4096 | bytes 16384
  387.6 0.3 reshape.306
  388.2 0.5 all_to_all.17
  388.7 5.2 %fusion.1 = f32[1024]{0:T(1024)S(1)} fusion(bf16[1024,4096]{0,1:T(8,128)(2,1)} %all-gather.6.cloned.1.call-done), kind=kLoop, calls=%fused_computation.7 | loop fusion | flops 12581888 | bytes 8392704 | tf_op jit(solution)/shard_map/reduce_sum | solution.py:113
  394.0 0.5 copy-done.2
  394.5 2.5 fusion.17
  (69 shorter events, 3.0 us)
Async XLA Ops:
  6.5 157.7 %copy-start = (bf16[2048,256]{1,0:T(8,128)(2,1)S(1)}, bf16[2048,256]{1,0:T(8,128)(2,1)}, u32[]{:S(2)}) copy-start(bf16[2048,256]{1,0:T(8,128)(2,1)} %param.19) | copy-start | bytes 3145732
  6.5 153.4 %all-gather.4.cloned.1.call-start = ((), (), s32[]{:S(2)}) async-start(), calls=%async_computation.1 | async-start | bytes 4259840 | tf_op jit(solution)/shard_map/all_gather | solution.py:42
  7.3 381.4 %all-gather.6.cloned.1.call-start = ((), (), s32[]{:S(2)}) async-start(), calls=%async_computation.2 | async-start | bytes 8519680 | tf_op jit(solution)/shard_map/all_gather | solution.py:108
  164.3 3.8 copy-start.1
  164.3 3.8 copy-start.3
  169.0 5.8 %collective-permute-start.1 = (bf16[3,320]{0,1:T(8,128)(2,1)S(1)}, bf16[3,320]{0,1:T(8,128)(2,1)S(1)}, u32[]{:S(2)}, u32[]{:S(2)}) collective-permute-start(bf16[3,320]{0,1:T(8,128)(2,1)S(1)} %pad_maximum_fusion.2), channel_id=1, source_target_pairs={{0,64},{64,128},{128,192},{192,256},{256,320},{320,384},{384,448},... | collective-permute-start | bytes 5768 | tf_op jit(solution)/shard_map/ppermute | solution.py:12
  176.2 46.5 %copy-start.4 = (bf16[2048,64]{0,1:T(8,128)(2,1)S(1)}, bf16[2048,64]{0,1:T(8,128)(2,1)}, u32[]{:S(2)}) copy-start(bf16[2048,64]{0,1:T(8,128)(2,1)} %param.17) | copy-start | bytes 786436
  185.4 41.1 %copy-start.5 = (bf16[64,2048]{1,0:T(8,128)(2,1)S(1)}, bf16[64,2048]{1,0:T(8,128)(2,1)}, u32[]{:S(2)}) copy-start(bf16[64,2048]{1,0:T(8,128)(2,1)} %param.27) | copy-start | bytes 786436
  185.4 5.4 %collective-permute-start = (f32[1,64,128]{2,1,0:T(8,128)S(1)}, f32[1,64,128]{2,1,0:T(8,128)S(1)}, u32[]{:S(2)}, u32[]{:S(2)}) collective-permute-start(f32[1,64,128]{2,1,0:T(8,128)S(1)} %multiply_add_fusion.2), channel_id=1, source_target_pairs={{0,64},{64,128},{128,192},{192,256},{256,320},{320,384},{384,448},... | collective-permute-start | bytes 98312 | tf_op jit(solution)/shard_map/while/body/eval_jaxpr/ppermute | solution.py:12
  190.8 5.2 %collective-permute-start = (f32[1,64,128]{2,1,0:T(8,128)S(1)}, f32[1,64,128]{2,1,0:T(8,128)S(1)}, u32[]{:S(2)}, u32[]{:S(2)}) collective-permute-start(f32[1,64,128]{2,1,0:T(8,128)S(1)} %multiply_add_fusion.2), channel_id=1, source_target_pairs={{0,64},{64,128},{128,192},{192,256},{256,320},{320,384},{384,448},... | collective-permute-start | bytes 98312 | tf_op jit(solution)/shard_map/while/body/eval_jaxpr/ppermute | solution.py:12
  196.0 5.2 %collective-permute-start = (f32[1,64,128]{2,1,0:T(8,128)S(1)}, f32[1,64,128]{2,1,0:T(8,128)S(1)}, u32[]{:S(2)}, u32[]{:S(2)}) collective-permute-start(f32[1,64,128]{2,1,0:T(8,128)S(1)} %multiply_add_fusion.2), channel_id=1, source_target_pairs={{0,64},{64,128},{128,192},{192,256},{256,320},{320,384},{384,448},... | collective-permute-start | bytes 98312 | tf_op jit(solution)/shard_map/while/body/eval_jaxpr/ppermute | solution.py:12
  201.3 5.2 %collective-permute-start = (f32[1,64,128]{2,1,0:T(8,128)S(1)}, f32[1,64,128]{2,1,0:T(8,128)S(1)}, u32[]{:S(2)}, u32[]{:S(2)}) collective-permute-start(f32[1,64,128]{2,1,0:T(8,128)S(1)} %multiply_add_fusion.2), channel_id=1, source_target_pairs={{0,64},{64,128},{128,192},{192,256},{256,320},{320,384},{384,448},... | collective-permute-start | bytes 98312 | tf_op jit(solution)/shard_map/while/body/eval_jaxpr/ppermute | solution.py:12
  206.5 5.2 %collective-permute-start = (f32[1,64,128]{2,1,0:T(8,128)S(1)}, f32[1,64,128]{2,1,0:T(8,128)S(1)}, u32[]{:S(2)}, u32[]{:S(2)}) collective-permute-start(f32[1,64,128]{2,1,0:T(8,128)S(1)} %multiply_add_fusion.2), channel_id=1, source_target_pairs={{0,64},{64,128},{128,192},{192,256},{256,320},{320,384},{384,448},... | collective-permute-start | bytes 98312 | tf_op jit(solution)/shard_map/while/body/eval_jaxpr/ppermute | solution.py:12
  211.7 5.2 %collective-permute-start = (f32[1,64,128]{2,1,0:T(8,128)S(1)}, f32[1,64,128]{2,1,0:T(8,128)S(1)}, u32[]{:S(2)}, u32[]{:S(2)}) collective-permute-start(f32[1,64,128]{2,1,0:T(8,128)S(1)} %multiply_add_fusion.2), channel_id=1, source_target_pairs={{0,64},{64,128},{128,192},{192,256},{256,320},{320,384},{384,448},... | collective-permute-start | bytes 98312 | tf_op jit(solution)/shard_map/while/body/eval_jaxpr/ppermute | solution.py:12
  217.0 5.2 %collective-permute-start = (f32[1,64,128]{2,1,0:T(8,128)S(1)}, f32[1,64,128]{2,1,0:T(8,128)S(1)}, u32[]{:S(2)}, u32[]{:S(2)}) collective-permute-start(f32[1,64,128]{2,1,0:T(8,128)S(1)} %multiply_add_fusion.2), channel_id=1, source_target_pairs={{0,64},{64,128},{128,192},{192,256},{256,320},{320,384},{384,448},... | collective-permute-start | bytes 98312 | tf_op jit(solution)/shard_map/while/body/eval_jaxpr/ppermute | solution.py:12
  222.4 17.6 %copy-start.6 = (bf16[64]{0:T(256)(128)(2,1)S(1)}, bf16[64]{0:T(256)(128)(2,1)}, u32[]{:S(2)}) copy-start(bf16[64]{0:T(256)(128)(2,1)} %param.26) | copy-start | bytes 388
  227.8 159.8 %all-to-all-start = ((bf16[64,2,1024]{2,1,0:T(2,128)(2,1)}), bf16[64,2,1024]{2,1,0:T(2,128)(2,1)S(1)}, u32[]{:S(2)}, u32[]{:S(2)}) async-start(bf16[64,2,1024]{2,1,0:T(2,128)(2,1)} %reshape.305), calls=%async_computation | async-start | bytes 524288 | tf_op jit(solution)/shard_map/all_to_all | solution.py:106
  388.7 5.8 %copy-start.2 = (bf16[1024,4096]{0,1:T(8,128)(2,1)S(1)}, bf16[1024,4096]{0,1:T(8,128)(2,1)}, u32[]{:S(2)}) copy-start(bf16[1024,4096]{0,1:T(8,128)(2,1)} %all-gather.6.cloned.1.call-done) | copy-start | bytes 25165828
Sparse Core Ops, SparseCore 0:
  10.3 149.6 all-gather.3
  226.6 154.3 all-gather.5
where the time goes:
time: 404 us
  waiting for transfers between devices  176 us (44%)
  blocking collectives  147 us (36%)
  starting transfers between devices  25.8 us (6%)
  between operations  16.4 us (4%)
  matrix products  14.6 us (4%)
  other arithmetic  10.6 us (3%)
  local copies, waits for them, and re-layouts  10.1 us (2%)
    all_gather x1, waiting for transfers between devices, body(): piece = lax.all_gather(tokens, 'head', axis=1, tiled=True)  149 us
    unnamed x1, blocking collectives  147 us
    ppermute x8, waiting for transfers between devices, from_behind(): return lax.ppermute(block, axis, route)  26.6 us
    ppermute x8, starting transfers between devices, from_behind(): return lax.ppermute(block, axis, route)  15.4 us
    dot_general x4, matrix products, product(): return jnp.dot(piece, weight, preferred_element_type=jnp.float32)  11.1 us
    all_to_all x1, starting transfers between devices, body(): lax.all_to_all(out_weight, 'head', split_axis=1, concat_axis=0, tiled=True)  10.3 us
  transfers between devices with their start and end apart: 11, of which 9 were waited for; matrix products, arithmetic and copies ran while one was open for 1% of the time, Pallas kernels for 0%

commit v1 on v0

--- a/solution.py
+++ b/solution.py
@@ -39,7 +39,9 @@
     inner_width = x_weight.shape[1]
     head_size = inner_width // heads_here
     state_size = bc_weight.shape[1] // 2
-    piece = lax.all_gather(tokens, "head", axis=1, tiled=True)
+    piece = jnp.concatenate(
+        lax.all_to_all(jnp.stack([tokens] * lax.axis_size("head")), "head", 0, 0), axis=1
+    )
 
     def product(weight):
         return jnp.dot(piece, weight, preferred_element_type=jnp.float32)

time: 404 us -> 461 us (1.14)
  waiting for transfers between devices: 176 us -> 214 us
  starting transfers between devices: 25.8 us -> 40.4 us
    all_to_all x0 -> x1, waiting for transfers between devices: none -> 188 us  [body(): lax.all_to_all(jnp.stack([tokens] * lax.axis_size('head')), 'head', 0, 0)]
    all_gather x1 -> x0, waiting for transfers between devices: 149 us -> none  [body(): piece = lax.all_gather(tokens, 'head', axis=1, tiled=True)]
    all_to_all x0 -> x1, starting transfers between devices: none -> 19 us  [body(): lax.all_to_all(jnp.stack([tokens] * lax.axis_size('head')), 'head', 0, 0)]
where the time goes in v1:
time: 461 us
  waiting for transfers between devices  214 us (46%)
  blocking collectives  148 us (32%)
  starting transfers between devices  40.4 us (9%)
  matrix products  16.6 us (4%)
  between operations  16.4 us (4%)
  local copies, waits for them, and re-layouts  11.9 us (3%)
  other arithmetic  10.6 us (2%)
    all_to_all x1, waiting for transfers between devices, body(): lax.all_to_all(jnp.stack([tokens] * lax.axis_size('head')), 'head', 0, 0)  188 us
    unnamed x1, blocking collectives  148 us
    ppermute x8, waiting for transfers between devices, from_behind(): return lax.ppermute(block, axis, route)  26.6 us
    all_to_all x1, starting transfers between devices, body(): lax.all_to_all(jnp.stack([tokens] * lax.axis_size('head')), 'head', 0, 0)  19 us
    ppermute x8, starting transfers between devices, from_behind(): return lax.ppermute(block, axis, route)  15.4 us
    dot_general x4, matrix products, product(): return jnp.dot(piece, weight, preferred_element_type=jnp.float32)  13.1 us
  transfers between devices with their start and end apart: 11, of which 9 were waited for; matrix products, arithmetic and copies ran while one was open for 1% of the time, Pallas kernels for 0%

profile of v1, /device:TPU:10, one launch (start us, length us, event | category | flops | bytes accessed | tf_op | source)
XLA Modules:
  0.0 460.7 jit_solution(2028875510062490540)
XLA Ops:
  6.5 3.4 stack.2
  10.0 19.0 %all-to-all-start = ((bf16[64,1024,32]{1,2,0:T(8,128)(2,1)}), bf16[64,1024,32]{1,2,0:T(8,128)(2,1)}, u32[]{:S(2)}, u32[]{:S(2)}) async-start(bf16[64,1024,32]{1,2,0:T(8,128)(2,1)} %stack.2), calls=%async_computation | async-start | bytes 8388608 | tf_op jit(solution)/shard_map/all_to_all | solution.py:43
  31.1 187.8 %all-to-all-done = bf16[64,1024,32]{1,2,0:T(8,128)(2,1)} async-done(((bf16[64,1024,32]{1,2,0:T(8,128)(2,1)}), bf16[64,1024,32]{1,2,0:T(8,128)(2,1)}, u32[]{:S(2)}, u32[]{:S(2)}) %all-to-all-start) | async-done | bytes 4194336 | tf_op jit(solution)/shard_map/all_to_all | solution.py:43
  218.9 2.8 fusion.45
  221.7 1.2 reduce-window.6
  223.2 3.5 convolution_convert_fusion
  226.8 3.0 convolution_convert_fusion.2
  230.0 1.9 collective-permute-start.1
  232.2 3.5 collective-permute-done.1
  235.7 1.0 multiply_convert_fusion
  237.1 0.3 convert_multiply_fusion.2
  237.7 8.1 %while.28 = (s32[]{:T(128)}, f32[1,64,128]{2,1,0:T(8,128)S(1)}, f32[1]{0:T(128)}, f32[4,1,64,128]{3,2,1,0:T(8,128)S(1)}, f32[4,1]{0,1:T(1,128)S(1)}, /*index=5*/...) while((s32[]{:T(128)}, f32[1,64,128]{2,1,0:T(8,128)S(1)}, f32[1]{0:T(128)}, ...), condition=%wide.region_3.4_spmd.clone, body=%wide.region_2.3_spmd.clone.sunk | while | flops 32772 | bytes 164008 | solution.py:89
  237.8 0.6 constant_dynamic-slice_fusion.2
  238.4 0.7 bitcast_add_fusion.4
  239.8 0.6 constant_dynamic-slice_fusion.2
  240.3 0.7 bitcast_add_fusion.4
  241.8 0.6 constant_dynamic-slice_fusion.2
  242.4 0.7 bitcast_add_fusion.4
  243.8 0.6 constant_dynamic-slice_fusion.2
  244.4 0.7 bitcast_add_fusion.4
  245.8 0.5 fusion.10
  246.4 36.8 %while.27 = (s32[]{:T(128)}, f32[1,64,128]{2,1,0:T(8,128)S(1)}, f32[1]{0:T(128)}, f32[1,64,128]{2,1,0:T(8,128)S(1)}, s32[]{:T(128)}) while((s32[]{:T(128)}, f32[1,64,128]{2,1,0:T(8,128)S(1)}, f32[1]{0:T(128)}, f32[1,64,128]{2,1,0:T(8,128)S(1)}, s32[]{:T(128)}) %tuple.53), condition=%wide.region_5.6_spmd, body=%wide.region_4.5_spmd.sunk | while | flops 16386 | bytes 229481 | solution.py:96
  246.4 2.1 collective-permute-start
  248.4 3.3 collective-permute-done
  251.8 1.9 collective-permute-start
  253.7 3.3 collective-permute-done
  257.0 1.9 collective-permute-start
  258.9 3.3 collective-permute-done
  262.2 1.9 collective-permute-start
  264.1 3.3 collective-permute-done
  267.4 1.9 collective-permute-start
  269.4 3.3 collective-permute-done
  272.7 1.9 collective-permute-start
  274.6 3.3 collective-permute-done
  277.9 1.9 collective-permute-start
  279.8 3.3 collective-permute-done
  283.1 0.3 fusion.12
  283.6 3.7 multiply_convert_fusion.1
  287.4 0.3 copy.64
  287.7 1.0 reshape.315
  288.7 6.0 %all-to-all-start.1 = ((bf16[64,2,1024]{2,1,0:T(2,128)(2,1)}), bf16[64,2,1024]{2,1,0:T(2,128)(2,1)S(1)}, u32[]{:S(2)}, u32[]{:S(2)}) async-start(bf16[64,2,1024]{2,1,0:T(2,128)(2,1)} %reshape.315), calls=%async_computation.1 | async-start | bytes 524288 | tf_op jit(solution)/shard_map/all_to_all | solution.py:108
  294.7 1.3 dynamic-slice
  296.9 147.5 %all-reduce = bf16[4096]{0:T(1024)(128)(2,1)S(1)} all-reduce(bf16[4096]{0:T(1024)(128)(2,1)S(1)} %dynamic-update-slice), channel_id=2, replica_groups=mesh['seq'=8,'head'=64] {'head'}, use_global_device_ids=true, to_apply=%add | all-reduce | flops 4096 | bytes 16384
  444.4 0.3 reshape.316
  445.0 0.5 all_to_all.21
  445.5 5.2 %fusion.1 = f32[1024]{0:T(1024)S(1)} fusion(bf16[1024,4096]{0,1:T(8,128)(2,1)} %all-gather.3.cloned.1.call-done), kind=kLoop, calls=%fused_computation.7 | loop fusion | flops 12581888 | bytes 8392704 | tf_op jit(solution)/shard_map/reduce_sum | solution.py:115
  450.8 0.5 copy-done.1
  451.3 2.5 fusion.17
  (73 shorter events, 2.8 us)
Async XLA Ops:
  6.5 216.6 %copy-start = (bf16[2048,256]{1,0:T(8,128)(2,1)S(1)}, bf16[2048,256]{1,0:T(8,128)(2,1)}, u32[]{:S(2)}) copy-start(bf16[2048,256]{1,0:T(8,128)(2,1)} %param.19) | copy-start | bytes 3145732
  10.0 21.1 %copy-start.7 = (f32[4,64]{1,0:T(4,128)S(1)}, f32[4,64]{1,0:T(4,128)}, u32[]{:S(2)}) copy-start(f32[4,64]{1,0:T(4,128)} %param.21) | copy-start | bytes 3076
  10.0 21.1 %copy-start.6 = (f32[4,256]{1,0:T(4,128)S(1)}, f32[4,256]{1,0:T(4,128)}, u32[]{:S(2)}) copy-start(f32[4,256]{1,0:T(4,128)} %param.22) | copy-start | bytes 12292
  10.0 208.9 %copy-start.5 = (bf16[2048,1]{0,1:T(2,128)(2,1)S(1)}, bf16[2048,1]{0,1:T(2,128)(2,1)}, u32[]{:S(2)}) copy-start(bf16[2048,1]{0,1:T(2,128)(2,1)} %param.20) | copy-start | bytes 12292
  10.0 208.9 %all-to-all-start = ((bf16[64,1024,32]{1,2,0:T(8,128)(2,1)}), bf16[64,1024,32]{1,2,0:T(8,128)(2,1)}, u32[]{:S(2)}, u32[]{:S(2)}) async-start(bf16[64,1024,32]{1,2,0:T(8,128)(2,1)} %stack.2), calls=%async_computation | async-start | bytes 8388608 | tf_op jit(solution)/shard_map/all_to_all | solution.py:43
  28.9 416.6 %all-gather.3.cloned.1.call-start = ((), (), s32[]{:S(2)}) async-start(), calls=%async_computation.2 | async-start | bytes 8519680 | tf_op jit(solution)/shard_map/all_gather | solution.py:110
  223.2 3.6 copy-start.2
  230.0 5.8 %collective-permute-start.1 = (bf16[3,320]{0,1:T(8,128)(2,1)S(1)}, bf16[3,320]{0,1:T(8,128)(2,1)S(1)}, u32[]{:S(2)}, u32[]{:S(2)}) collective-permute-start(bf16[3,320]{0,1:T(8,128)(2,1)S(1)} %pad_maximum_fusion.2), channel_id=1, source_target_pairs={{0,64},{64,128},{128,192},{192,256},{256,320},{320,384},{384,448},... | collective-permute-start | bytes 5768 | tf_op jit(solution)/shard_map/ppermute | solution.py:12
  237.1 46.5 %copy-start.3 = (bf16[2048,64]{0,1:T(8,128)(2,1)S(1)}, bf16[2048,64]{0,1:T(8,128)(2,1)}, u32[]{:S(2)}) copy-start(bf16[2048,64]{0,1:T(8,128)(2,1)} %param.17) | copy-start | bytes 786436
  246.3 41.1 %copy-start.4 = (bf16[64,2048]{1,0:T(8,128)(2,1)S(1)}, bf16[64,2048]{1,0:T(8,128)(2,1)}, u32[]{:S(2)}) copy-start(bf16[64,2048]{1,0:T(8,128)(2,1)} %param.27) | copy-start | bytes 786436
  246.4 5.4 %collective-permute-start = (f32[1,64,128]{2,1,0:T(8,128)S(1)}, f32[1,64,128]{2,1,0:T(8,128)S(1)}, u32[]{:S(2)}, u32[]{:S(2)}) collective-permute-start(f32[1,64,128]{2,1,0:T(8,128)S(1)} %multiply_add_fusion.2), channel_id=1, source_target_pairs={{0,64},{64,128},{128,192},{192,256},{256,320},{320,384},{384,448},... | collective-permute-start | bytes 98312 | tf_op jit(solution)/shard_map/while/body/eval_jaxpr/ppermute | solution.py:12
  251.8 5.2 %collective-permute-start = (f32[1,64,128]{2,1,0:T(8,128)S(1)}, f32[1,64,128]{2,1,0:T(8,128)S(1)}, u32[]{:S(2)}, u32[]{:S(2)}) collective-permute-start(f32[1,64,128]{2,1,0:T(8,128)S(1)} %multiply_add_fusion.2), channel_id=1, source_target_pairs={{0,64},{64,128},{128,192},{192,256},{256,320},{320,384},{384,448},... | collective-permute-start | bytes 98312 | tf_op jit(solution)/shard_map/while/body/eval_jaxpr/ppermute | solution.py:12
  257.0 5.2 %collective-permute-start = (f32[1,64,128]{2,1,0:T(8,128)S(1)}, f32[1,64,128]{2,1,0:T(8,128)S(1)}, u32[]{:S(2)}, u32[]{:S(2)}) collective-permute-start(f32[1,64,128]{2,1,0:T(8,128)S(1)} %multiply_add_fusion.2), channel_id=1, source_target_pairs={{0,64},{64,128},{128,192},{192,256},{256,320},{320,384},{384,448},... | collective-permute-start | bytes 98312 | tf_op jit(solution)/shard_map/while/body/eval_jaxpr/ppermute | solution.py:12
  262.2 5.2 %collective-permute-start = (f32[1,64,128]{2,1,0:T(8,128)S(1)}, f32[1,64,128]{2,1,0:T(8,128)S(1)}, u32[]{:S(2)}, u32[]{:S(2)}) collective-permute-start(f32[1,64,128]{2,1,0:T(8,128)S(1)} %multiply_add_fusion.2), channel_id=1, source_target_pairs={{0,64},{64,128},{128,192},{192,256},{256,320},{320,384},{384,448},... | collective-permute-start | bytes 98312 | tf_op jit(solution)/shard_map/while/body/eval_jaxpr/ppermute | solution.py:12
  267.4 5.2 %collective-permute-start = (f32[1,64,128]{2,1,0:T(8,128)S(1)}, f32[1,64,128]{2,1,0:T(8,128)S(1)}, u32[]{:S(2)}, u32[]{:S(2)}) collective-permute-start(f32[1,64,128]{2,1,0:T(8,128)S(1)} %multiply_add_fusion.2), channel_id=1, source_target_pairs={{0,64},{64,128},{128,192},{192,256},{256,320},{320,384},{384,448},... | collective-permute-start | bytes 98312 | tf_op jit(solution)/shard_map/while/body/eval_jaxpr/ppermute | solution.py:12
  272.7 5.2 %collective-permute-start = (f32[1,64,128]{2,1,0:T(8,128)S(1)}, f32[1,64,128]{2,1,0:T(8,128)S(1)}, u32[]{:S(2)}, u32[]{:S(2)}) collective-permute-start(f32[1,64,128]{2,1,0:T(8,128)S(1)} %multiply_add_fusion.2), channel_id=1, source_target_pairs={{0,64},{64,128},{128,192},{192,256},{256,320},{320,384},{384,448},... | collective-permute-start | bytes 98312 | tf_op jit(solution)/shard_map/while/body/eval_jaxpr/ppermute | solution.py:12
  277.9 5.2 %collective-permute-start = (f32[1,64,128]{2,1,0:T(8,128)S(1)}, f32[1,64,128]{2,1,0:T(8,128)S(1)}, u32[]{:S(2)}, u32[]{:S(2)}) collective-permute-start(f32[1,64,128]{2,1,0:T(8,128)S(1)} %multiply_add_fusion.2), channel_id=1, source_target_pairs={{0,64},{64,128},{128,192},{192,256},{256,320},{320,384},{384,448},... | collective-permute-start | bytes 98312 | tf_op jit(solution)/shard_map/while/body/eval_jaxpr/ppermute | solution.py:12
  283.4 13.2 %copy-start.8 = (bf16[64]{0:T(256)(128)(2,1)S(1)}, bf16[64]{0:T(256)(128)(2,1)}, u32[]{:S(2)}) copy-start(bf16[64]{0:T(256)(128)(2,1)} %param.26) | copy-start | bytes 388
  288.7 155.7 %all-to-all-start.1 = ((bf16[64,2,1024]{2,1,0:T(2,128)(2,1)}), bf16[64,2,1024]{2,1,0:T(2,128)(2,1)S(1)}, u32[]{:S(2)}, u32[]{:S(2)}) async-start(bf16[64,2,1024]{2,1,0:T(2,128)(2,1)} %reshape.315), calls=%async_computation.1 | async-start | bytes 524288 | tf_op jit(solution)/shard_map/all_to_all | solution.py:108
  445.5 5.8 %copy-start.1 = (bf16[1024,4096]{0,1:T(8,128)(2,1)S(1)}, bf16[1024,4096]{0,1:T(8,128)(2,1)}, u32[]{:S(2)}) copy-start(bf16[1024,4096]{0,1:T(8,128)(2,1)} %all-gather.3.cloned.1.call-done) | copy-start | bytes 25165828
Sparse Core Ops, SparseCore 0:
  287.5 149.4 all-gather.2
